TPU v7x, 32 devices: a whole 2x2x4 slice. The times are simulated.
32 devices in a mesh: groups: 2 (over x), row: 4 (over z), col: 4 (over y, core).
Axes of the slice: x: 2, y: 2, z: 4, core: 2. Of those that a mesh axis runs over, the one named last changes fastest.
Arguments:
- src_feats: bfloat16 [32768, 256], P(('groups', 'row', 'col')), parts along dimension 0, may hold values from -6 to 6
- dst_feats: bfloat16 [32768, 256], P(('groups', 'col', 'row')), parts along dimension 0, may hold values from -6 to 6
- w_self: bfloat16 [256, 256], replicated, may hold values from -0.375 to 0.375
- w_neigh: bfloat16 [256, 256], replicated, may hold values from -0.375 to 0.375
- bias: float32 [256], replicated, may hold values from -2.5 to 2.5
- cotangent: bfloat16 [32768, 256], P(('groups', 'col', 'row')), parts along dimension 0, may hold values from -6 to 6
- tile_vals: bfloat16 [8, 4, 32, 128, 128], P(('groups', 'col'), 'row'), parts along dimension 0
- tile_rows: int32 [8, 4, 32], P(('groups', 'col'), 'row'), parts along dimension 0, may hold values from 0 to 31
- tile_cols: int32 [8, 4, 32], P(('groups', 'col'), 'row'), parts along dimension 0, may hold values from 0 to 31
- tile_count: int32 [8, 4], P(('groups', 'col'), 'row'), parts along dimension 0, may hold values from 6 to 32, as said below
Outputs:
- hidden_out: bfloat16 [32768, 256], P(('groups', 'col', 'row')), parts along dimension 0
- grad_src: bfloat16 [32768, 256], P(('groups', 'row', 'col')), parts along dimension 0
- grad_dst: bfloat16 [32768, 256], P(('groups', 'col', 'row')), parts along dimension 0
- grad_w_self: float32 [512, 256], P('groups'), parts along dimension 0
- grad_w_neigh: float32 [512, 256], P('groups'), parts along dimension 0
- grad_bias: float32 [512], P('groups'), parts along dimension 0
There are 2 independent parts, one for each index of `groups`. A program takes and returns all parts, laid end to end along the dimension named above; an argument that names none is the same for every part. Nothing has to cross between parts.
Inputs may be any that keep to these rules, and one draw needn't show every extreme that they name: `tile_count`: live slots of a cell, those before its count, name distinct tile positions; the largest count is exactly 32 in every draw.
All inputs are finite; a program needn't handle non-finite values.
Results may differ from a plain program's by a relative error of at most 0.009.
Values may be sent and summed in bfloat16 or wider, within the bound.
A program may use at most 128 MiB of HBM per device.

v0:
```python
import math

import jax
import jax.numpy as jnp
from jax import lax
from jax.sharding import PartitionSpec as P


def accumulate(tile_vals, out_index, in_index, live_count, source, out_blocks, flipped):
    tile_size = tile_vals.shape[-1]
    feature_width = source.shape[1]
    slot_total = tile_vals.shape[0]
    blocks = source.reshape(-1, tile_size, feature_width)
    group_size = min(32, slot_total)
    einsum_form = "tji,tjf->tif" if flipped else "tij,tjf->tif"

    def add_group(group_number, totals):
        first = group_number * group_size
        part_vals = lax.dynamic_slice_in_dim(tile_vals, first, group_size, 0)
        part_in = lax.dynamic_slice_in_dim(in_index, first, group_size, 0)
        part_out = lax.dynamic_slice_in_dim(out_index, first, group_size, 0)
        live = first + jnp.arange(group_size, dtype=jnp.int32) < live_count
        part_vals = jnp.where(live[:, None, None], part_vals, jnp.zeros((), part_vals.dtype))
        gathered = jnp.take(blocks, part_in, axis=0)
        product = jnp.einsum(einsum_form, part_vals, gathered, preferred_element_type=jnp.float32)
        return totals.at[part_out].add(product)

    initial = jnp.zeros((out_blocks, tile_size, feature_width), jnp.float32)
    turn_count = slot_total // group_size
    totals = lax.fori_loop(0, turn_count, add_group, initial)
    return totals.reshape(out_blocks * tile_size, feature_width)


def rounded_term(values):
    narrow = lax.optimization_barrier(values.astype(jnp.bfloat16))
    return narrow.astype(jnp.float32)


def dense_step(dst_rows, agg_rows, cot_rows, w_self, w_neigh, bias):
    preact = jnp.dot(dst_rows, w_self, preferred_element_type=jnp.float32)
    preact = preact + jnp.dot(agg_rows, w_neigh, preferred_element_type=jnp.float32) + bias
    gate_sig = jax.nn.sigmoid(preact)
    hidden_rows = (preact * gate_sig).astype(jnp.bfloat16)
    slope = gate_sig * (1.0 + preact * (1.0 - gate_sig))
    grad_rows = (cot_rows.astype(jnp.float32) * slope).astype(jnp.bfloat16)
    return (hidden_rows, grad_rows)


def local(
    src_feats,
    dst_feats,
    w_self,
    w_neigh,
    bias,
    cotangent,
    tile_vals,
    tile_rows,
    tile_cols,
    tile_count,
):
    cell_vals = tile_vals[0, 0]
    cell_rows = tile_rows[0, 0]
    cell_cols = tile_cols[0, 0]
    live_count = tile_count[0, 0]
    tile_size = cell_vals.shape[-1]
    own_rows = dst_feats.shape[0]
    row_blocks = own_rows * lax.axis_size("row") // tile_size
    col_blocks = src_feats.shape[0] * lax.axis_size("col") // tile_size
    source_block = lax.all_gather(src_feats, "col", axis=0, tiled=True)
    partial_value = rounded_term(
        accumulate(cell_vals, cell_rows, cell_cols, live_count, source_block, row_blocks, False)
    )
    aggregate = lax.psum_scatter(
        partial_value.astype(jnp.bfloat16), "row", scatter_dimension=0, tiled=True
    )
    hidden_out, grad_pre = dense_step(dst_feats, aggregate, cotangent, w_self, w_neigh, bias)
    back_own = jnp.dot(grad_pre, w_neigh.T, preferred_element_type=jnp.float32).astype(jnp.bfloat16)
    back_feats = lax.all_gather(back_own, "row", axis=0, tiled=True)
    grad_dst = jnp.dot(grad_pre, w_self.T, preferred_element_type=jnp.float32).astype(jnp.bfloat16)
    back_partial = rounded_term(
        accumulate(cell_vals, cell_cols, cell_rows, live_count, back_feats, col_blocks, True)
    )
    grad_src = lax.psum_scatter(
        back_partial.astype(jnp.bfloat16), "col", scatter_dimension=0, tiled=True
    )
    term_self = jnp.dot(dst_feats.T, grad_pre, preferred_element_type=jnp.float32)
    term_neigh = jnp.dot(aggregate.T, grad_pre, preferred_element_type=jnp.float32)
    term_bias = jnp.sum(grad_pre.astype(jnp.float32), axis=0)
    sum_self, sum_neigh, sum_bias = lax.psum((term_self, term_neigh, term_bias), ("row", "col"))
    scaling = 1.0 / math.sqrt(own_rows * lax.axis_size("row") * lax.axis_size("col"))
    return (
        hidden_out,
        grad_src,
        grad_dst,
        sum_self * scaling,
        sum_neigh * scaling,
        sum_bias * scaling,
    )


def solution(mesh):
    return jax.shard_map(
        local,
        mesh=mesh,
        in_specs=(
            P(("groups", "row", "col"), None),
            P(("groups", "col", "row"), None),
            P(),
            P(),
            P(),
            P(("groups", "col", "row"), None),
            P(("groups", "col"), "row", None, None, None),
            P(("groups", "col"), "row", None),
            P(("groups", "col"), "row", None),
            P(("groups", "col"), "row"),
        ),
        out_specs=(
            P(("groups", "col", "row"), None),
            P(("groups", "row", "col"), None),
            P(("groups", "col", "row"), None),
            P("groups", None),
            P("groups", None),
            P("groups"),
        ),
        check_vma=False,
    )
```

profile of v0, /device:TPU:0, one launch (start us, length us, event | category | flops | bytes accessed | tf_op | source)
XLA Modules:
  0.0 285.3 jit_solution(16710576952648079957)
XLA Ops:
  7.2 0.0 copy-start
  7.2 0.0 all-gather.3.cloned.1.call-start
  7.2 0.7 all-gather.3.cloned.1.call-update
  7.9 0.0 reduce-scatter.3.cloned.1.call-start
  8.6 0.7 compare_select_fusion.1
  9.3 0.7 fusion.9
  9.9 0.7 compare_and_fusion.1
  10.6 24.3 %all-gather.3.cloned.1.call-done = bf16[4096,256]{1,0:T(8,128)(2,1)} async-done(((bf16[1024,256]{1,0:T(8,128)(2,1)}), bf16[4096,256]{1,0:T(8,128)(2,1)}) %all-gather.3.cloned.1.call-update) | async-done | bytes 2097168 | tf_op jit(solution)/shard_map/all_gather | solution.py:69
  34.9 2.3 gather_fusion
  37.2 4.0 %fusion.2 = f32[32,128,256]{2,1,0:T(8,128)} fusion(bf16[32,128,256]{2,1,0:T(8,128)(2,1)S(1)} %gather_fusion, pred[32]{0:T(512)(128)(4,1)S(1)} %get-tuple-element.66, bf16[1,1,32,128,128]{4,3,2,1,0:T(8,128)(2,1)} %param.18, pred[32]{0:T(512)(128)(4,1)S(1)} %get-tuple-element.67), kind=kOutput, calls=%fused_computation.6 | convolution fusion | flops 270008320 | bytes 7340096 | tf_op jit(solution)/shard_map/while/body/eval_jaxpr/tij,tjf->tif/dot_general | solution.py:25
  41.2 2.4 broadcast.57.clone
  43.6 9.8 %scatter_fusion = f32[32,128,256]{2,1,0:T(8,128)} fusion(f32[32,128,256]{2,1,0:T(8,128)} %broadcast.57.clone, s32[32]{0:T(128)S(1)} %fusion.9, f32[32,128,256]{2,1,0:T(8,128)} %fusion.2), kind=kCustom, calls=%fused_computation.2 | custom fusion | flops 1048576 | bytes 12583040 | tf_op jit(solution)/shard_map/while/body/eval_jaxpr/scatter-add | solution.py:26
  53.4 3.8 %convert_element_type.34 = bf16[32,128,256]{2,1,0:T(8,128)(2,1)} convert(f32[32,128,256]{2,1,0:T(8,128)} %scatter_fusion) | non-fusion elementwise | flops 1048576 | bytes 6291456 | tf_op jit(solution)/shard_map/convert_element_type | solution.py:35
  57.2 0.0 reduce-scatter.3.cloned.1.call-update
  57.2 0.0 all-gather.5.cloned.1.call-start
  57.3 0.0 copy-done
  57.3 0.8 copy-done.2
  58.1 0.3 fusion.15
  58.4 0.0 copy-start.7
  58.4 0.0 copy-start.4
  58.4 43.0 %reduce-scatter.3.cloned.1.call-done = bf16[1024,256]{1,0:T(8,128)(2,1)} async-done(((bf16[4096,256]{1,0:T(8,128)(2,1)}), bf16[1024,256]{1,0:T(8,128)(2,1)}) %reduce-scatter.3.cloned.1.call-update) | async-done | bytes 524304 | tf_op jit(solution)/shard_map/reduce_scatter | solution.py:73
  101.4 0.0 copy-done.3
  101.4 0.0 copy-done.6
  101.4 2.5 convert_reduce_fusion
  104.0 1.1 convolution_convert_fusion.1
  105.1 0.0 all-gather.5.cloned.1.call-update
  105.1 0.0 all-reduce.3.cloned.1.call-start
  105.2 0.0 copy-done.7
  105.2 1.0 convolution_bitcast_fusion
  106.3 1.1 fusion.16
  107.3 0.0 all-reduce.3.cloned.1.call-update
  107.4 0.0 reduce-scatter.5.cloned.1.call-start
  107.4 43.2 %all-gather.5.cloned.1.call-done = bf16[4096,256]{1,0:T(8,128)(2,1)} async-done(((bf16[1024,256]{1,0:T(8,128)(2,1)}), bf16[4096,256]{1,0:T(8,128)(2,1)}) %all-gather.5.cloned.1.call-update) | async-done | bytes 2097168 | tf_op jit(solution)/shard_map/all_gather | solution.py:78
  150.6 2.3 gather_fusion.1
  152.9 4.3 %fusion = f32[32,128,256]{2,1,0:T(8,128)} fusion(bf16[32,128,256]{2,1,0:T(8,128)(2,1)S(1)} %gather_fusion.1, pred[32]{0:T(512)(128)(4,1)S(1)} %compare_and_fusion, bf16[1,1,32,128,128]{4,3,2,1,0:T(8,128)(2,1)} %param.18, pred[32]{0:T(512)(128)(4,1)S(1)} %get-tuple-element.67), kind=kOutput, calls=%fused_computation.4 | convolution fusion | flops 270008320 | bytes 7340096 | tf_op jit(solution)/shard_map/while/body/eval_jaxpr/tji,tjf->tif/dot_general | solution.py:25
  157.2 2.4 broadcast.57
  159.6 9.8 %scatter_fusion.1 = f32[32,128,256]{2,1,0:T(8,128)} fusion(f32[32,128,256]{2,1,0:T(8,128)} %broadcast.57, s32[32]{0:T(128)S(1)} %fusion.10, f32[32,128,256]{2,1,0:T(8,128)} %fusion), kind=kCustom, calls=%fused_computation.3 | custom fusion | flops 1048576 | bytes 12583040 | tf_op jit(solution)/shard_map/while/body/eval_jaxpr/scatter-add | solution.py:26
  169.4 3.8 %convert_element_type.40 = bf16[32,128,256]{2,1,0:T(8,128)(2,1)} convert(f32[32,128,256]{2,1,0:T(8,128)} %scatter_fusion.1) | non-fusion elementwise | flops 1048576 | bytes 6291456 | tf_op jit(solution)/shard_map/convert_element_type | solution.py:35
  173.3 0.0 reduce-scatter.5.cloned.1.call-update
  173.3 31.4 %psum.23 = f32[256]{0:T(256)S(1)} all-reduce(f32[256]{0:T(256)S(1)} %get-tuple-element.55), channel_id=1, replica_groups=mesh['groups'=2,'row'=4,'col'=4] {'row','col'}, use_global_device_ids=true, to_apply=%region_7.9 | all-reduce | flops 256 | bytes 2048 | tf_op jit(solution)/shard_map/psum | solution.py:89
  204.7 0.6 broadcast_multiply_fusion.2
  205.3 1.1 convolution_convert_fusion
  206.4 37.3 %all-reduce.3.cloned.1.call-done = (f32[256,256]{0,1:T(8,128)}, f32[256,256]{0,1:T(8,128)}) async-done(((f32[256,256]{0,1:T(8,128)}, f32[256,256]{0,1:T(8,128)}), (f32[256,256]{0,1:T(8,128)}, f32[256,256]{0,1:T(8,128)})) %all-reduce.3.cloned.1.call-update) | async-done | bytes 524304 | tf_op jit(solution)/shard_map/psum | solution.py:89
  243.7 1.0 broadcast_multiply_fusion.1
  244.7 0.8 copy.18
  245.5 1.0 broadcast_multiply_fusion
  246.5 0.8 copy.19
  247.3 31.5 %reduce-scatter.5.cloned.1.call-done = bf16[1024,256]{1,0:T(8,128)(2,1)} async-done(((bf16[4096,256]{1,0:T(8,128)(2,1)}), bf16[1024,256]{1,0:T(8,128)(2,1)}) %reduce-scatter.5.cloned.1.call-update) | async-done | bytes 524304 | tf_op jit(solution)/shard_map/reduce_scatter | solution.py:83
  (13 shorter events, 0.0 us)
Async XLA Ops:
  7.2 50.1 %copy-start = (bf16[1024,256]{1,0:T(8,128)(2,1)S(1)}, bf16[1024,256]{1,0:T(8,128)(2,1)}, u32[]{:S(2)}) copy-start(bf16[1024,256]{1,0:T(8,128)(2,1)} %param.13) | copy-start | bytes 1572868
  7.2 27.7 %all-gather.3.cloned.1.call-start = ((), (), s32[]{:S(2)}) async-start(), calls=%async_computation.2 | async-start | bytes 2621440 | tf_op jit(solution)/shard_map/all_gather | solution.py:69
  7.9 93.5 %reduce-scatter.3.cloned.1.call-start = ((), (), s32[]{:S(2)}) async-start(), calls=%async_computation.3 | async-start | bytes 2621440 | tf_op jit(solution)/shard_map/reduce_scatter | solution.py:73
  57.2 0.9 copy-start.2
  57.2 44.2 %copy-start.3 = (bf16[256,256]{1,0:T(8,128)(2,1)S(1)}, bf16[256,256]{1,0:T(8,128)(2,1)}, u32[]{:S(2)}) copy-start(bf16[256,256]{1,0:T(8,128)(2,1)} %param.15) | copy-start | bytes 393220
  57.2 44.2 %copy-start.5 = (bf16[1024,256]{1,0:T(8,128)(2,1)S(1)}, bf16[1024,256]{1,0:T(8,128)(2,1)}, u32[]{:S(2)}) copy-start(bf16[1024,256]{1,0:T(8,128)(2,1)} %param.17) | copy-start | bytes 1572868
  57.2 44.2 %copy-start.6 = (f32[256]{0:T(256)S(1)}, f32[256]{0:T(256)}, u32[]{:S(2)}) copy-start(f32[256]{0:T(256)} %param.16) | copy-start | bytes 3076
  57.2 93.4 %all-gather.5.cloned.1.call-start = ((), (), s32[]{:S(2)}) async-start(), calls=%async_computation.4 | async-start | bytes 2621440 | tf_op jit(solution)/shard_map/all_gather | solution.py:78
  58.4 46.8 %copy-start.7 = (s32[1,1,32]{2,1,0:T(1,128)S(1)}, s32[1,1,32]{2,1,0:T(1,128)}, u32[]{:S(2)}) copy-start(s32[1,1,32]{2,1,0:T(1,128)} %param.19) | copy-start | bytes 388
  58.4 46.8 %copy-start.4 = (s32[1,1,32]{2,1,0:T(1,128)S(1)}, s32[1,1,32]{2,1,0:T(1,128)}, u32[]{:S(2)}) copy-start(s32[1,1,32]{2,1,0:T(1,128)} %param.20) | copy-start | bytes 388
  104.0 2.3 copy-start.1
  105.1 138.6 %all-reduce.3.cloned.1.call-start = ((), (), s32[]{:S(2)}) async-start(), calls=%async_computation.6 | async-start | bytes 1048576 | tf_op jit(solution)/shard_map/psum | solution.py:89
  107.4 171.4 %reduce-scatter.5.cloned.1.call-start = ((), (), s32[]{:S(2)}) async-start(), calls=%async_computation.5 | async-start | bytes 2621440 | tf_op jit(solution)/shard_map/reduce_scatter | solution.py:83
Sparse Core Ops, SparseCore 0:
  9.6 25.2 all-gather.2
  57.3 44.0 reduce-scatter.2
  105.2 45.3 all-gather.4
  154.9 88.8 all-reduce.2
  246.8 31.9 reduce-scatter.4
where the time goes:
time: 286 us; the launch traced here: 285 us
  waiting for transfers between devices  180 us (63%)
  other arithmetic  31.8 us (11%)
  blocking collectives  31.4 us (11%)
  matrix products  15.4 us (5%)
  between operations  14.5 us (5%)
  local copies, waits for them, and re-layouts  11.9 us (4%)
    all_gather x1, waiting for transfers between devices, local(): back_feats = lax.all_gather(back_own, 'row', axis=0, tiled=True)  43.2 us
    reduce_scatter x1, waiting for transfers between devices, local(): lax.psum_scatter(partial_value.astype(jnp.bfloat16), 'row', scatter_dimen...  43 us
    psum x1, waiting for transfers between devices, local(): lax.psum((term_self, term_neigh, term_bias), ('row', 'col'))  37.3 us
    reduce_scatter x1, waiting for transfers between devices, local(): lax.psum_scatter(back_partial.astype(jnp.bfloat16), 'col', scatter_dimens...  31.5 us
    psum x1, blocking collectives, local(): lax.psum((term_self, term_neigh, term_bias), ('row', 'col'))  31.4 us
    all_gather x1, waiting for transfers between devices, local(): source_block = lax.all_gather(src_feats, 'col', axis=0, tiled=True)  24.3 us
    scatter-add x2, other arithmetic, add_group(): return totals.at[part_out].add(product)  19.6 us
    dot_general x2, matrix products, add_group(): jnp.einsum(einsum_form, part_vals, gathered, preferred_element_type=jnp.f...  8.27 us
  transfers between devices with their start and end apart: 5, of which 5 were waited for; matrix products, arithmetic and copies ran while one was open for 11% of the time, Pallas kernels for 0%

commit v1 on v0

--- a/solution.py
+++ b/solution.py
@@ -1,9 +1,15 @@
+import functools
 import math
 
 import jax
 import jax.numpy as jnp
 from jax import lax
+from jax.experimental import pallas as pl
+from jax.experimental.pallas import tpu as pltpu
 from jax.sharding import PartitionSpec as P
+
+MESH = pl.DeviceIdType.MESH
+CHUNKS = 4
 
 
 def accumulate(tile_vals, out_index, in_index, live_count, source, out_blocks, flipped):
@@ -98,9 +104,476 @@
     )
 
 
+def sage_kernel(
+    sizes, scaling, idx, src, dst_hbm, w_self, w_neigh, bias, cot_hbm, vals_hbm,
+    hidden, grad_src, grad_dst, grads,
+    dst, cot, vals, gathered, sums, part, from_low, from_high, back, grads_in,
+    back_part, pair_in, chip_in, term_acc, terms, terms_in, terms_row,
+    load_sem, src_send, src_recv, fwd_send, red_send, up_recv, down_recv,
+    own_send, pass_send, back_recv, pair_send, pair_recv, chip_send, chip_recv,
+    t1_send, t1_recv, t2_send, t2_recv, t3_send, t3_recv,
+):
+    rows_n, cols_n, slots, blocks, chunks, piece = sizes
+    chips_n = cols_n // 2
+    per = blocks // chunks
+    tile = src.shape[1]
+    width = src.shape[2]
+    row_blocks = rows_n * blocks
+    col_blocks = cols_n * blocks
+    z = lax.axis_index("row")
+    c = lax.axis_index("col")
+    chip = c // 2
+    core = c % 2
+    sibling = chip * 2 + (1 - core)
+    f32, bf16 = jnp.float32, jnp.bfloat16
+
+    def remote(src_ref, dst_ref, send, recv, device):
+        return pltpu.make_async_remote_copy(
+            src_ref=src_ref, dst_ref=dst_ref, send_sem=send, recv_sem=recv,
+            device_id=device, device_id_type=MESH,
+        )
+
+    loads = [
+        pltpu.make_async_copy(src, gathered.at[pl.ds(c * blocks, blocks)], load_sem.at[0]),
+        pltpu.make_async_copy(vals_hbm, vals, load_sem.at[1]),
+        pltpu.make_async_copy(dst_hbm, dst, load_sem.at[2]),
+        pltpu.make_async_copy(cot_hbm, cot, load_sem.at[3]),
+    ]
+    for load in loads:
+        load.start()
+
+    barrier = pltpu.get_barrier_semaphore()
+    for k in range(1, cols_n):
+        pl.semaphore_signal(barrier, inc=1, device_id={"col": lax.rem(c + k, cols_n)}, device_id_type=MESH)
+    for k in range(1, rows_n):
+        pl.semaphore_signal(barrier, inc=1, device_id={"row": lax.rem(z + k, rows_n)}, device_id_type=MESH)
+    pl.semaphore_wait(barrier, cols_n + rows_n - 2)
+
+    def src_copy(owner, k, sem_at, device, first):
+        at = pl.ds(owner * blocks + k * per, per)
+        from_ref = src.at[pl.ds(k * per, per)] if first else gathered.at[at]
+        return remote(from_ref, gathered.at[at], src_send.at[sem_at, k], src_recv.at[owner, k], {"col": device})
+
+    def far(dy):
+        return lax.rem(chip + dy, chips_n) * 2 + core
+
+    for k in range(chunks):
+        for dy in range(1, chips_n):
+            src_copy(c, k, dy, far(dy), True).start()
+    for k in range(chunks):
+        src_copy(c, k, 0, sibling, True).start()
+
+    def src_pass(dy, k):
+        owner = far(dy)
+        at = pl.ds(owner * blocks + k * per, per)
+        return remote(gathered.at[at], gathered.at[at], fwd_send.at[dy, k], src_recv.at[owner, k], {"col": sibling})
+
+    sums[slots] = jnp.zeros((tile, width), f32)
+    term_acc[...] = jnp.zeros_like(term_acc)
+
+    for k in range(chunks):
+        for dy in range(1, chips_n):
+            src_copy(far(dy), k, dy, sibling, False).wait_recv()
+            src_pass(dy, k).start()
+    for load in loads[:2]:
+        load.wait()
+    for k in range(chunks):
+        for y in range(chips_n):
+            src_copy(y * 2 + 1 - core, k, 0, sibling, False).wait_recv()
+
+    def forward_slot(s, carry):
+        product = jnp.dot(vals[s], gathered[idx[1, s]], preferred_element_type=f32)
+        sums[s] = product + sums[idx[2, s]]
+        return carry
+
+    lax.fori_loop(0, slots, forward_slot, 0)
+
+    def forward_row(i, carry):
+        part[i] = sums[idx[4, i]].astype(bf16)
+        return carry
+
+    lax.fori_loop(0, row_blocks, forward_row, 0)
+
+    def at_of(d, k):
+        return pl.ds(d * blocks + k * per, per)
+
+    def up_copy(d, k, device):
+        return remote(part.at[at_of(d, k)], from_low.at[at_of(d, k)], red_send.at[d, k], up_recv.at[d, k], {"row": device})
+
+    def down_copy(d, k, device):
+        return remote(part.at[at_of(d, k)], from_high.at[at_of(d, k)], red_send.at[d, k], down_recv.at[d, k], {"row": device})
+
+    next_up = lax.rem(z + 1, rows_n)
+    next_down = lax.rem(z + rows_n - 1, rows_n)
+
+    def add_in(d, k, buf):
+        at = at_of(d, k)
+        part[at] = (part[at].astype(f32) + buf[at].astype(f32)).astype(bf16)
+
+    def send_up(k):
+        def step(i, carry):
+            d = rows_n - 1 - i
+
+            @pl.when(z > 0)
+            def _():
+                up_copy(d, k, next_up).wait_recv()
+                add_in(d, k, from_low)
+
+            up_copy(d, k, next_up).start()
+            return carry
+
+        lax.fori_loop(0, rows_n - 1 - z, step, 0)
+
+    def send_down(k):
+        def step(d, carry):
+            @pl.when(z < rows_n - 1)
+            def _():
+                down_copy(d, k, next_down).wait_recv()
+                add_in(d, k, from_high)
+
+            down_copy(d, k, next_down).start()
+            return carry
+
+        lax.fori_loop(0, z, step, 0)
+
+    is_end = jnp.logical_or(z == 0, z == rows_n - 1)
+    is_low = z < rows_n // 2
+
+    def stage_a(k):
+        @pl.when(is_low)
+        def _():
+            send_up(k)
+
+        @pl.when(jnp.logical_not(is_low))
+        def _():
+            send_down(k)
+
+    def stage_b(k):
+        @pl.when(is_low)
+        def _():
+            send_down(k)
+
+        @pl.when(jnp.logical_not(is_low))
+        def _():
+            send_up(k)
+
+    @pl.when(is_end)
+    def _():
+        def each(k, carry):
+            stage_a(k)
+            return carry
+
+        lax.fori_loop(0, chunks, each, 0)
+
+    for load in loads[2:]:
+        load.wait()
+
+    def own_copy(k, way, device):
+        at = at_of(z, k)
+        return remote(back.at[at], back.at[at], own_send.at[way, k], back_recv.at[z, k], {"row": device})
+
+    def pass_copy(owner, k, device):
+        at = at_of(owner, k)
+        return remote(back.at[at], back.at[at], pass_send.at[owner, k], back_recv.at[owner, k], {"row": device})
+
+    def finish(k):
+        @pl.when(z > 0)
+        def _():
+            up_copy(z, k, next_up).wait_recv()
+            add_in(z, k, from_low)
+
+        @pl.when(z < rows_n - 1)
+        def _():
+            down_copy(z, k, next_down).wait_recv()
+            add_in(z, k, from_high)
+
+        at = pl.ds(k * per, per)
+        flat = (per * tile, width)
+        agg_rows = part[at_of(z, k)].reshape(flat)
+        dst_rows = dst[at].reshape(flat)
+        preact = jnp.dot(dst_rows, w_self[...], preferred_element_type=f32)
+        preact = preact + jnp.dot(agg_rows, w_neigh[...], preferred_element_type=f32) + bias[...]
+        gate_sig = jax.nn.sigmoid(preact)
+        slope = gate_sig * (1.0 + preact * (1.0 - gate_sig))
+        grad_rows = (cot[at].reshape(flat).astype(f32) * slope).astype(bf16)
+        turned = (((1,), (1,)), ((), ()))
+        back_rows = lax.dot_general(grad_rows, w_neigh[...], turned, preferred_element_type=f32)
+        back[at_of(z, k)] = back_rows.astype(bf16).reshape((per, tile, width))
+
+        @pl.when(z < rows_n - 1)
+        def _():
+            own_copy(k, 0, next_up).start()
+
+        @pl.when(z > 0)
+        def _():
+            own_copy(k, 1, next_down).start()
+
+        hidden[at] = (preact * gate_sig).astype(bf16).reshape((per, tile, width))
+        dst_grad = lax.dot_general(grad_rows, w_self[...], turned, preferred_element_type=f32)
+        grad_dst[at] = dst_grad.astype(bf16).reshape((per, tile, width))
+        outer = (((0,), (0,)), ((), ()))
+        term_acc[pl.ds(0, width)] += lax.dot_general(dst_rows, grad_rows, outer, preferred_element_type=f32)
+        term_acc[pl.ds(width, width)] += lax.dot_general(agg_rows, grad_rows, outer, preferred_element_type=f32)
+        term_acc[pl.ds(2 * width, 8)] += jnp.sum(grad_rows.astype(f32).reshape((per * tile // 8, 8, width)), axis=0)
+
+    def pass_on(j, k):
+        @pl.when(jnp.logical_and(z >= j, z < rows_n - 1))
+        def _():
+            copy = pass_copy(z - j, k, next_up)
+            copy.wait_recv()
+            copy.start()
+
+        @pl.when(jnp.logical_and(z + j < rows_n, z > 0))
+        def _():
+            copy = pass_copy(z + j, k, next_down)
+            copy.wait_recv()
+            copy.start()
+
+    def turn(t, carry):
+        @pl.when(jnp.logical_and(t < chunks, jnp.logical_not(is_end)))
+        def _():
+            stage_a(t)
+
+        @pl.when(jnp.logical_and(t >= 1, t <= chunks))
+        def _():
+            stage_b(t - 1)
+            finish(t - 1)
+
+        for j in range(1, rows_n - 1):
+            @pl.when(jnp.logical_and(t >= 1 + j, t <= chunks + j))
+            def _():
+                pass_on(j, t - 1 - j)
+
+        return carry
+
+    lax.fori_loop(0, chunks + 1, turn, 0)
+
+    bias_sum = jnp.sum(term_acc[pl.ds(2 * width, 8)], axis=0, keepdims=True)
+    spot = lax.broadcasted_iota(jnp.int32, (16, width), 0) == 0
+    terms[pl.ds(0, 2 * width)] = term_acc[...][: 2 * width].astype(bf16)
+    terms[pl.ds(2 * width, 16)] = jnp.where(spot, bias_sum, 0.0).astype(bf16)
+    if cols_n * piece > 2 * width + 16:
+        rest = cols_n * piece - 2 * width - 16
+        terms[pl.ds(2 * width + 16, rest)] = jnp.zeros((rest, width), bf16)
+
+    def t1_copy(k):
+        peer = lax.rem(c + k, cols_n)
+        return remote(terms.at[pl.ds(peer * piece, piece)], terms_in.at[k - 1], t1_send.at[k - 1], t1_recv.at[k - 1], {"col": peer})
+
+    def t2_copy(k):
+        peer = lax.rem(z + k, rows_n)
+        return remote(terms_row.at[z], terms_row.at[z], t2_send.at[k - 1], t2_recv.at[k - 1], {"row": peer})
+
+    def t3_copy(k):
+        peer = lax.rem(c + k, cols_n)
+        at = pl.ds(c * piece, piece)
+        return remote(grads_in.at[at], grads_in.at[at], t3_send.at[k - 1], t3_recv.at[k - 1], {"col": peer})
+
+    for k in range(1, cols_n):
+        t1_copy(k).start()
+
+    lax.fori_loop(chunks + 1, chunks + rows_n - 1, turn, 0)
+
+    total = terms[pl.ds(c * piece, piece)].astype(f32)
+    for k in range(1, cols_n):
+        t1_copy(k).wait_recv()
+        total = total + terms_in[k - 1].astype(f32)
+    terms_row[z] = total.astype(bf16)
+    for k in range(1, rows_n):
+        t2_copy(k).start()
+
+    @pl.when(z == rows_n - 1)
+    def _():
+        for owner in range(rows_n - 1):
+            for k in range(chunks):
+                pass_copy(owner, k, next_down).wait_recv()
+
+    @pl.when(z == 0)
+    def _():
+        for owner in range(1, rows_n):
+            for k in range(chunks):
+                pass_copy(owner, k, next_up).wait_recv()
+
+    for k in range(1, rows_n):
+        t2_copy(k).wait_recv()
+    whole = terms_row[0].astype(f32)
+    for k in range(1, rows_n):
+        whole = whole + terms_row[k].astype(f32)
+    grads_in[pl.ds(c * piece, piece)] = whole * scaling
+    for k in range(1, cols_n):
+        t3_copy(k).start()
+
+    def backward_slot(s, carry):
+        product = lax.dot_general(vals[s], back[idx[0, s]], (((0,), (0,)), ((), ())), preferred_element_type=f32)
+        sums[s] = product + sums[idx[3, s]]
+        return carry
+
+    lax.fori_loop(0, slots, backward_slot, 0)
+
+    def backward_block(owner):
+        def each(i, carry):
+            at = owner * blocks + i
+            back_part[at] = sums[idx[5, at]].astype(bf16)
+            return carry
+
+        lax.fori_loop(0, blocks, each, 0)
+
+    def pair_copy(dy, k):
+        y = lax.rem(chip + dy, chips_n)
+        owner = y * 2 + 1 - core
+        return remote(
+            back_part.at[at_of(owner, k)], pair_in.at[at_of(dy, k)],
+            pair_send.at[dy, k], pair_recv.at[dy, k], {"col": sibling},
+        )
+
+    def chip_copy(dy, k):
+        return remote(
+            back_part.at[at_of(far(dy), k)], chip_in.at[at_of(dy, k)],
+            chip_send.at[dy, k], chip_recv.at[dy, k], {"col": far(dy)},
+        )
+
+    order = list(range(1, chips_n)) + [0]
+    for dy in order:
+        backward_block(lax.rem(chip + dy, chips_n) * 2 + 1 - core)
+        for k in range(chunks):
+            pair_copy(dy, k).start()
+        backward_block(far(dy))
+    for dy in order:
+        for k in range(chunks):
+            pair_copy(dy, k).wait_recv()
+            at = at_of(far(dy), k)
+            back_part[at] = (back_part[at].astype(f32) + pair_in[at_of(dy, k)].astype(f32)).astype(bf16)
+            if dy:
+                chip_copy(dy, k).start()
+    for k in range(chunks):
+        summed = back_part[at_of(c, k)].astype(f32)
+        for dy in range(1, chips_n):
+            chip_copy(dy, k).wait_recv()
+            summed = summed + chip_in[at_of(dy, k)].astype(f32)
+        grad_src[pl.ds(k * per, per)] = summed.astype(bf16)
+
+    for k in range(1, cols_n):
+        t3_copy(k).wait_recv()
+    grads[...] = grads_in[...]
+
+    for k in range(chunks):
+        src_copy(c, k, 0, sibling, True).wait_send()
+        for dy in range(1, chips_n):
+            src_copy(c, k, dy, far(dy), True).wait_send()
+            src_pass(dy, k).wait_send()
+            chip_copy(dy, k).wait_send()
+        for dy in range(chips_n):
+            pair_copy(dy, k).wait_send()
+        for d in range(rows_n):
+            @pl.when(z != d)
+            def _():
+                up_copy(d, k, next_up).wait_send()
+
+        @pl.when(z < rows_n - 1)
+        def _():
+            own_copy(k, 0, next_up).wait_send()
+
+        @pl.when(z > 0)
+        def _():
+            own_copy(k, 1, next_down).wait_send()
+
+        for d in range(rows_n):
+            @pl.when(jnp.logical_and(z != d, jnp.logical_not(is_end)))
+            def _():
+                pass_copy(d, k, next_up).wait_send()
+    for k in range(1, cols_n):
+        t1_copy(k).wait_send()
+        t3_copy(k).wait_send()
+    for k in range(1, rows_n):
+        t2_copy(k).wait_send()
+
+
+def slot_links(keys, live, blocks):
+    slots = keys.shape[0]
+    place = jnp.arange(slots, dtype=jnp.int32)
+    same = (keys[:, None] == keys[None, :]) & live[None, :] & (place[None, :] < place[:, None])
+    before = jnp.max(jnp.where(same, place[None, :], -1), axis=1)
+    hit = (jnp.arange(blocks, dtype=jnp.int32)[:, None] == keys[None, :]) & live[None, :]
+    last = jnp.max(jnp.where(hit, place[None, :], -1), axis=1)
+    return jnp.where(before < 0, slots, before), jnp.where(last < 0, slots, last)
+
+
+def fused(src_feats, dst_feats, w_self, w_neigh, bias, cotangent, tile_vals, tile_rows, tile_cols, tile_count):
+    cell_vals, cell_rows, cell_cols = tile_vals[0, 0], tile_rows[0, 0], tile_cols[0, 0]
+    slots, tile = cell_vals.shape[:2]
+    own_rows, width = src_feats.shape
+    rows_n, cols_n = lax.axis_size("row"), lax.axis_size("col")
+    blocks = own_rows // tile
+    chunks = CHUNKS
+    row_blocks, col_blocks = rows_n * blocks, cols_n * blocks
+    piece = -(-(2 * width + 16) // (16 * cols_n)) * 16
+    live = jnp.arange(slots, dtype=jnp.int32) < tile_count[0, 0]
+    row_prev, row_last = slot_links(cell_rows, live, row_blocks)
+    col_prev, col_last = slot_links(cell_cols, live, col_blocks)
+    most = max(slots, row_blocks, col_blocks)
+    lists = (cell_rows, cell_cols, row_prev, col_prev, row_last, col_last)
+    idx = jnp.stack([jnp.pad(v, (0, most - v.shape[0])) for v in lists])
+    scaling = 1.0 / math.sqrt(own_rows * rows_n * cols_n)
+    sizes = (rows_n, cols_n, slots, blocks, chunks, piece)
+    bf16, f32 = jnp.bfloat16, jnp.float32
+    cube = lambda n: pltpu.VMEM((n, tile, width), bf16)
+    dma = lambda *shape: pltpu.SemaphoreType.DMA(shape)
+    chips_n = cols_n // 2
+    vmem = pl.BlockSpec(memory_space=pltpu.VMEM)
+    hbm = pl.BlockSpec(memory_space=pl.ANY)
+    smem = pl.BlockSpec(memory_space=pltpu.SMEM)
+    own = jax.ShapeDtypeStruct((blocks, tile, width), bf16)
+    split = lambda v: v.reshape(blocks, tile, width)
+    hidden, grad_src, grad_dst, grads = pl.pallas_call(
+        functools.partial(sage_kernel, sizes, scaling),
+        out_shape=(own, own, own, jax.ShapeDtypeStruct((cols_n * piece, width), f32)),
+        in_specs=[smem, hbm, hbm, vmem, vmem, vmem, hbm, hbm],
+        out_specs=(vmem, vmem, vmem, vmem),
+        scratch_shapes=[
+            cube(blocks), cube(blocks), pltpu.VMEM((slots, tile, tile), bf16),
+            cube(col_blocks), pltpu.VMEM((slots + 1, tile, width), f32),
+            cube(row_blocks), cube(row_blocks), cube(row_blocks), cube(row_blocks),
+            pltpu.VMEM((cols_n * piece, width), f32),
+            cube(col_blocks), cube(chips_n * blocks), cube(chips_n * blocks),
+            pltpu.VMEM((2 * width + 16, width), f32),
+            pltpu.VMEM((cols_n * piece, width), bf16),
+            pltpu.VMEM((cols_n - 1, piece, width), bf16),
+            pltpu.VMEM((rows_n, piece, width), bf16),
+            dma(4), dma(chips_n, chunks), dma(cols_n, chunks), dma(chips_n, chunks),
+            dma(rows_n, chunks), dma(rows_n, chunks), dma(rows_n, chunks),
+            dma(2, chunks), dma(rows_n, chunks), dma(rows_n, chunks),
+            dma(chips_n, chunks), dma(chips_n, chunks), dma(chips_n, chunks), dma(chips_n, chunks),
+            dma(cols_n - 1), dma(cols_n - 1), dma(rows_n - 1), dma(rows_n - 1), dma(cols_n - 1), dma(cols_n - 1),
+        ],
+        compiler_params=pltpu.CompilerParams(
+            collective_id=0, has_side_effects=True, vmem_limit_bytes=50 * 2**20
+        ),
+        name="sage",
+    )(idx, split(src_feats), split(dst_feats), w_self, w_neigh, bias[None, :], split(cotangent), cell_vals)
+    flat = lambda v: v.reshape(own_rows, width)
+    return (
+        flat(hidden), flat(grad_src), flat(grad_dst),
+        grads[:width], grads[width : 2 * width], grads[2 * width],
+    )
+
+
+def fits(own_rows, width, slots, tile):
+    rows_n, cols_n = lax.axis_size("row"), lax.axis_size("col")
+    block = own_rows * width * 2
+    planned = block * (4 * rows_n + 3 * cols_n + 5) + slots * tile * (tile * 2 + width * 4)
+    even = cols_n % 2 == 0 and rows_n > 1 and cols_n > 2
+    return even and own_rows % (tile * CHUNKS) == 0 and planned < 40 * 2**20
+
+
+def chosen(*args):
+    slots, tile = args[6].shape[2:4]
+    body = fused if fits(*args[0].shape, slots, tile) else local
+    return body(*args)
+
+
 def solution(mesh):
     return jax.shard_map(
-        local,
+        chosen,
         mesh=mesh,
         in_specs=(
             P(("groups", "row", "col"), None),

time: 286 us -> 137 us (0.48)
  waiting for transfers between devices: 180 us -> 0 us
  Pallas kernels: 0 us -> 125 us
  other arithmetic: 31.8 us -> 0.23 us
  blocking collectives: 31.4 us -> 0 us
  matrix products: 15.4 us -> 0 us
  between operations: 14.5 us -> 1.34 us
    pallas_call x0 -> x1, Pallas kernels: none -> 125 us  [fused(): pl.pallas_call(functools.partial(sage_kernel, sizes, scaling), out_shape=...]
    reduce_scatter x2 -> x0, waiting for transfers between devices: 74.5 us -> none  [the longest x1 43 us: local(): lax.psum_scatter(partial_value.astype(jnp.bfloat16), 'row', scatter_dimen...]
    all_gather x2 -> x0, waiting for transfers between devices: 67.5 us -> none  [the longest x1 43.2 us: local(): back_feats = lax.all_gather(back_own, 'row', axis=0, tiled=True)]
    psum x1 -> x0, waiting for transfers between devices: 37.3 us -> none  [local(): lax.psum((term_self, term_neigh, term_bias), ('row', 'col'))]
    psum x1 -> x0, blocking collectives: 31.4 us -> none  [local(): lax.psum((term_self, term_neigh, term_bias), ('row', 'col'))]
    scatter-add x2 -> x0, other arithmetic: 19.6 us -> none  [add_group(): return totals.at[part_out].add(product)]
    dot_general x8 -> x0, matrix products: 15.4 us -> none  [the longest x2 8.27 us: add_group(): jnp.einsum(einsum_form, part_vals, gathered, preferred_element_type=jnp.f...]
    convert_element_type x2 -> x0, other arithmetic: 7.61 us -> none  [rounded_term(): narrow = lax.optimization_barrier(values.astype(jnp.bfloat16))]
  transfers between devices with their start and end apart: 5 -> 0, of which waited for: 5 -> 0; matrix products, arithmetic and copies ran while one was open for 11% -> 0% of each run, Pallas kernels for 0% -> 0%
where the time goes in v1:
time: 137 us
  Pallas kernels  125 us (91%)
  local copies, waits for them, and re-layouts  10.1 us (7%)
    pallas_call x1, Pallas kernels, fused(): pl.pallas_call(functools.partial(sage_kernel, sizes, scaling), out_shape=...  125 us
    unnamed x19, local copies, waits for them, and re-layouts  8.64 us

profile of v1, /device:TPU:0, one launch (start us, length us, event | category | flops | bytes accessed | tf_op | source)
XLA Modules:
  0.0 137.1 jit_solution(6682482479329277922)
XLA Ops:
  1.3 0.0 copy-start.6
  1.3 0.0 copy-start.7
  1.3 0.6 copy-done.6
  1.9 0.0 copy-done.7
  2.0 0.2 select_reduce_fusion
  2.2 0.0 copy-start.5
  2.2 0.7 copy-done.5
  2.9 0.0 copy-start
  2.9 1.0 copy-done
  4.0 0.0 copy-start.1
  4.0 1.0 copy-done.1
  5.0 0.0 copy-start.2
  5.0 1.0 copy-done.2
  6.0 0.0 copy-start.3
  6.0 0.9 copy-done.3
  6.9 0.0 copy-start.4
  6.9 0.9 copy-done.4
  7.9 125.4 %sage.1 = (bf16[8,128,256]{2,1,0:T(8,128)(2,1)S(1)}, bf16[8,128,256]{2,1,0:T(8,128)(2,1)S(1)}, bf16[8,128,256]{2,1,0:T(8,128)(2,1)S(1)}, f32[576,256]{1,0:T(8,128)S(1)}) custom-call(s32[6,32]{1,0:T(8,128)S(1)} %stack.15.idx, bf16[8,128,256]{2,1,0:T(8,128)(2,1)S(1)} %bitcast.26, bf16[8,128,256]{2,1,0:T(8,128)(2,1)S(1)} %bitcast.27, ...), custom_call_target="tpu_custom_call" | custom-call | tf_op jit(solution)/shard_map/sage/pallas_call | solution.py:527
  133.3 0.8 fusion.4
  134.1 0.6 slice.11
  134.7 0.8 copy.20
  135.5 0.8 copy.21
  136.3 0.8 copy.22
  (4 shorter events, 0.0 us)
Async XLA Ops:
  1.3 0.7 copy-start.6
  1.3 0.7 copy-start.7
  2.2 0.7 copy-start.5
  2.9 1.0 copy-start
  4.0 1.0 copy-start.1
  5.0 1.0 copy-start.2
  6.0 0.9 copy-start.3
  6.9 0.9 copy-start.4

commit v2 on v1

--- a/solution.py
+++ b/solution.py
@@ -9,7 +9,11 @@
 from jax.sharding import PartitionSpec as P
 
 MESH = pl.DeviceIdType.MESH
-CHUNKS = 4
+CHUNKS = 8
+FINISH_LAG = 2
+PASS_LAG = 1
+HOLD = 2
+UNROLL = 8
 
 
 def accumulate(tile_vals, out_index, in_index, live_count, source, out_blocks, flipped):
@@ -186,13 +190,13 @@
         sums[s] = product + sums[idx[2, s]]
         return carry
 
-    lax.fori_loop(0, slots, forward_slot, 0)
+    lax.fori_loop(0, slots, forward_slot, 0, unroll=UNROLL)
 
     def forward_row(i, carry):
         part[i] = sums[idx[4, i]].astype(bf16)
         return carry
 
-    lax.fori_loop(0, row_blocks, forward_row, 0)
+    lax.fori_loop(0, row_blocks, forward_row, 0, unroll=UNROLL)
 
     def at_of(d, k):
         return pl.ds(d * blocks + k * per, per)
@@ -218,6 +222,10 @@
             def _():
                 up_copy(d, k, next_up).wait_recv()
                 add_in(d, k, from_low)
+
+            @pl.when(k >= HOLD)
+            def _():
+                up_copy(d, k - HOLD, next_up).wait_send()
 
             up_copy(d, k, next_up).start()
             return carry
@@ -231,6 +239,10 @@
                 down_copy(d, k, next_down).wait_recv()
                 add_in(d, k, from_high)
 
+            @pl.when(k >= HOLD)
+            def _():
+                down_copy(d, k - HOLD, next_down).wait_send()
+
             down_copy(d, k, next_down).start()
             return carry
 
@@ -256,14 +268,6 @@
         @pl.when(jnp.logical_not(is_low))
         def _():
             send_up(k)
-
-    @pl.when(is_end)
-    def _():
-        def each(k, carry):
-            stage_a(k)
-            return carry
-
-        lax.fori_loop(0, chunks, each, 0)
 
     for load in loads[2:]:
         load.wait()
@@ -330,23 +334,32 @@
             copy.start()
 
     def turn(t, carry):
+        @pl.when(jnp.logical_and(t < chunks, is_end))
+        def _():
+            stage_a(t)
+
+        @pl.when(jnp.logical_and(t >= FINISH_LAG, t < chunks + FINISH_LAG))
+        def _():
+            finish(t - FINISH_LAG)
+
+        for j in reversed(range(1, rows_n - 1)):
+            lag = FINISH_LAG + j * PASS_LAG
+
+            @pl.when(jnp.logical_and(t >= lag, t < chunks + lag))
+            def _():
+                pass_on(j, t - lag)
+
+        @pl.when(jnp.logical_and(t >= 1, t < chunks + 1))
+        def _():
+            stage_b(t - 1)
+
         @pl.when(jnp.logical_and(t < chunks, jnp.logical_not(is_end)))
         def _():
             stage_a(t)
 
-        @pl.when(jnp.logical_and(t >= 1, t <= chunks))
-        def _():
-            stage_b(t - 1)
-            finish(t - 1)
-
-        for j in range(1, rows_n - 1):
-            @pl.when(jnp.logical_and(t >= 1 + j, t <= chunks + j))
-            def _():
-                pass_on(j, t - 1 - j)
-
         return carry
 
-    lax.fori_loop(0, chunks + 1, turn, 0)
+    lax.fori_loop(0, chunks + FINISH_LAG, turn, 0)
 
     bias_sum = jnp.sum(term_acc[pl.ds(2 * width, 8)], axis=0, keepdims=True)
     spot = lax.broadcasted_iota(jnp.int32, (16, width), 0) == 0
@@ -372,7 +385,7 @@
     for k in range(1, cols_n):
         t1_copy(k).start()
 
-    lax.fori_loop(chunks + 1, chunks + rows_n - 1, turn, 0)
+    lax.fori_loop(chunks + FINISH_LAG, chunks + FINISH_LAG + (rows_n - 2) * PASS_LAG, turn, 0)
 
     total = terms[pl.ds(c * piece, piece)].astype(f32)
     for k in range(1, cols_n):
@@ -408,7 +421,7 @@
         sums[s] = product + sums[idx[3, s]]
         return carry
 
-    lax.fori_loop(0, slots, backward_slot, 0)
+    lax.fori_loop(0, slots, backward_slot, 0, unroll=UNROLL)
 
     def backward_block(owner):
         def each(i, carry):
@@ -416,7 +429,7 @@
             back_part[at] = sums[idx[5, at]].astype(bf16)
             return carry
 
-        lax.fori_loop(0, blocks, each, 0)
+        lax.fori_loop(0, blocks, each, 0, unroll=UNROLL)
 
     def pair_copy(dy, k):
         y = lax.rem(chip + dy, chips_n)
@@ -464,7 +477,7 @@
             chip_copy(dy, k).wait_send()
         for dy in range(chips_n):
             pair_copy(dy, k).wait_send()
-        for d in range(rows_n):
+        for d in range(rows_n if k >= chunks - HOLD else 0):
             @pl.when(z != d)
             def _():
                 up_copy(d, k, next_up).wait_send()
@@ -546,7 +559,7 @@
             dma(cols_n - 1), dma(cols_n - 1), dma(rows_n - 1), dma(rows_n - 1), dma(cols_n - 1), dma(cols_n - 1),
         ],
         compiler_params=pltpu.CompilerParams(
-            collective_id=0, has_side_effects=True, vmem_limit_bytes=50 * 2**20
+            collective_id=0, has_side_effects=True, vmem_limit_bytes=61 * 2**20
         ),
         name="sage",
     )(idx, split(src_feats), split(dst_feats), w_self, w_neigh, bias[None, :], split(cotangent), cell_vals)

time: 137 us -> 117 us (0.85)
  Pallas kernels: 125 us -> 107 us
  local copies, waits for them, and re-layouts: 10.1 us -> 7.69 us
    pallas_call x1, Pallas kernels: 125 us -> 107 us  [fused(): pl.pallas_call(functools.partial(sage_kernel, sizes, scaling), out_shape=...]
    unnamed x19 -> x13, local copies, waits for them, and re-layouts: 8.64 us -> 3.91 us
where the time goes in v2:
time: 117 us; the launch traced here: 116 us
  Pallas kernels  107 us (91%)
  local copies, waits for them, and re-layouts  7.69 us (7%)
  between operations  1.34 us (1%)
    pallas_call x1, Pallas kernels, fused(): pl.pallas_call(functools.partial(sage_kernel, sizes, scaling), out_shape=...  107 us
    unnamed x13, local copies, waits for them, and re-layouts  3.91 us

profile of v2, /device:TPU:0, one launch (start us, length us, event | category | flops | bytes accessed | tf_op | source)
XLA Modules:
  0.0 116.5 jit_solution(6746609252242037375)
XLA Ops:
  1.3 0.0 copy-start.3
  1.3 0.0 copy-start.4
  1.3 0.6 copy-done.3
  1.9 0.0 copy-done.4
  2.0 0.2 select_reduce_fusion
  2.2 0.6 stack.15.idx
  2.8 107.2 %sage.1 = (bf16[8,128,256]{2,1,0:T(8,128)(2,1)}, bf16[8,128,256]{2,1,0:T(8,128)(2,1)}, bf16[8,128,256]{2,1,0:T(8,128)(2,1)}, f32[576,256]{1,0:T(8,128)}) custom-call(s32[6,32]{1,0:T(8,128)} %stack.15.idx, bf16[8,128,256]{2,1,0:T(8,128)(2,1)} %bitcast.27, bf16[8,128,256]{2,1,0:T(8,128)(2,1)} %bitcast.28, bf16[256,256]{1,0:T(8,128)(2,1)} %w_self.1, ...), custom_call_target="tpu_custom_call" | custom-call | tf_op jit(solution)/shard_map/sage/pallas_call | solution.py:540
  110.0 0.0 copy-start.2
  110.0 1.9 %fusion.4 = (f32[256,256]{1,0:T(8,128)}, f32[256,256]{1,0:T(8,128)}) fusion(f32[576,256]{1,0:T(8,128)} %get-tuple-element.13), kind=kLoop, calls=%fused_computation.16 | loop fusion | bytes 1048576 | tf_op jit(solution)/shard_map/slice | solution.py:569
  111.9 1.3 %slice.11 = f32[1,256]{1,0:T(1,128)} slice(f32[576,256]{1,0:T(8,128)} %get-tuple-element.13), slice={[512:513], [0:256]} | slice | bytes 2048 | tf_op jit(solution)/shard_map/slice | solution.py:569
  113.2 0.0 copy-done.2
  113.2 0.0 copy-start.1
  113.2 0.8 copy.20
  114.0 0.4 copy-done.1
  114.4 0.0 copy-start
  114.4 0.8 copy.21
  115.2 0.4 copy-done
  115.7 0.8 copy.22
  (3 shorter events, 0.0 us)
Async XLA Ops:
  1.3 0.7 copy-start.3
  1.3 0.7 copy-start.4
  110.0 3.2 %copy-start.2 = (bf16[8,128,256]{2,1,0:T(8,128)(2,1)S(1)}, bf16[8,128,256]{2,1,0:T(8,128)(2,1)}, u32[]{:S(2)}) copy-start(bf16[8,128,256]{2,1,0:T(8,128)(2,1)} %get-tuple-element.10) | copy-start | bytes 1572868
  113.2 1.2 %copy-start.1 = (bf16[8,128,256]{2,1,0:T(8,128)(2,1)S(1)}, bf16[8,128,256]{2,1,0:T(8,128)(2,1)}, u32[]{:S(2)}) copy-start(bf16[8,128,256]{2,1,0:T(8,128)(2,1)} %get-tuple-element.11) | copy-start | bytes 1572868
  114.4 1.2 %copy-start = (bf16[8,128,256]{2,1,0:T(8,128)(2,1)S(1)}, bf16[8,128,256]{2,1,0:T(8,128)(2,1)}, u32[]{:S(2)}) copy-start(bf16[8,128,256]{2,1,0:T(8,128)(2,1)} %get-tuple-element.12) | copy-start | bytes 1572868

commit v3 on v2

--- a/solution.py
+++ b/solution.py
@@ -110,7 +110,7 @@
 
 def sage_kernel(
     sizes, scaling, idx, src, dst_hbm, w_self, w_neigh, bias, cot_hbm, vals_hbm,
-    hidden, grad_src, grad_dst, grads,
+    hidden, grad_src, grad_dst, grads_self, grads_neigh, grads_bias,
     dst, cot, vals, gathered, sums, part, from_low, from_high, back, grads_in,
     back_part, pair_in, chip_in, term_acc, terms, terms_in, terms_row,
     load_sem, src_send, src_recv, fwd_send, red_send, up_recv, down_recv,
@@ -467,7 +467,9 @@
 
     for k in range(1, cols_n):
         t3_copy(k).wait_recv()
-    grads[...] = grads_in[...]
+    grads_self[...] = grads_in[pl.ds(0, width)]
+    grads_neigh[...] = grads_in[pl.ds(width, width)]
+    grads_bias[...] = grads_in[pl.ds(2 * width, 8)]
 
     for k in range(chunks):
         src_copy(c, k, 0, sibling, True).wait_send()
@@ -536,12 +538,13 @@
     hbm = pl.BlockSpec(memory_space=pl.ANY)
     smem = pl.BlockSpec(memory_space=pltpu.SMEM)
     own = jax.ShapeDtypeStruct((blocks, tile, width), bf16)
+    term = jax.ShapeDtypeStruct((width, width), f32)
     split = lambda v: v.reshape(blocks, tile, width)
-    hidden, grad_src, grad_dst, grads = pl.pallas_call(
+    hidden, grad_src, grad_dst, grads_self, grads_neigh, grads_bias = pl.pallas_call(
         functools.partial(sage_kernel, sizes, scaling),
-        out_shape=(own, own, own, jax.ShapeDtypeStruct((cols_n * piece, width), f32)),
+        out_shape=(own, own, own, term, term, jax.ShapeDtypeStruct((8, width), f32)),
         in_specs=[smem, hbm, hbm, vmem, vmem, vmem, hbm, hbm],
-        out_specs=(vmem, vmem, vmem, vmem),
+        out_specs=(vmem,) * 6,
         scratch_shapes=[
             cube(blocks), cube(blocks), pltpu.VMEM((slots, tile, tile), bf16),
             cube(col_blocks), pltpu.VMEM((slots + 1, tile, width), f32),
@@ -566,7 +569,7 @@
     flat = lambda v: v.reshape(own_rows, width)
     return (
         flat(hidden), flat(grad_src), flat(grad_dst),
-        grads[:width], grads[width : 2 * width], grads[2 * width],
+        grads_self, grads_neigh, grads_bias[0],
     )
 
 

time: 117 us -> 118 us (level)
    unnamed x13 -> x17, local copies, waits for them, and re-layouts: 3.91 us -> 6.65 us
    slice x2 -> x1, local copies, waits for them, and re-layouts: 3.17 us -> 1.26 us  [fused(): grads_bias[0]]
where the time goes in v3:
time: 118 us; the launch traced here: 117 us
  Pallas kernels  107 us (91%)
  local copies, waits for them, and re-layouts  8.52 us (7%)
  between operations  1.33 us (1%)
    pallas_call x1, Pallas kernels, fused(): pl.pallas_call(functools.partial(sage_kernel, sizes, scaling), out_shape=...  107 us
    unnamed x17, local copies, waits for them, and re-layouts  6.65 us

profile of v3, /device:TPU:0, one launch (start us, length us, event | category | flops | bytes accessed | tf_op | source)
XLA Modules:
  0.0 117.3 jit_solution(13043131211358128815)
XLA Ops:
  1.3 0.0 copy-start.4
  1.3 0.0 copy-start.5
  1.3 0.6 copy-done.4
  1.9 0.0 copy-done.5
  2.0 0.2 select_reduce_fusion
  2.2 0.6 stack.15.idx
  2.8 107.2 %sage.1 = (bf16[8,128,256]{2,1,0:T(8,128)(2,1)}, bf16[8,128,256]{2,1,0:T(8,128)(2,1)}, bf16[8,128,256]{2,1,0:T(8,128)(2,1)}, f32[256,256]{1,0:T(8,128)}, f32[256,256]{1,0:T(8,128)}, /*index=5*/f32[8,256]{1,0:T(8,128)}) custom-call(s32[6,32]{1,0:T(8,128)} %stack.15.idx, bf16[8,128,256]{2,1,0:T(8,128)(2,1)} %bitcast.27, bf16[8,128,256]{2,1,0:T(8,128)(2,1)} %bitcast.28, ...), custom_call_target="tpu_custom_call" | custom-call | tf_op jit(solution)/shard_map/sage/pallas_call | solution.py:543
  110.0 1.3 %slice.3 = f32[1,256]{1,0:T(1,128)} slice(f32[8,256]{1,0:T(8,128)} %get-tuple-element.17), slice={[0:1], [0:256]} | slice | bytes 2048 | tf_op jit(solution)/shard_map/slice | solution.py:572
  111.3 0.0 copy-start.1
  111.3 1.9 %copy.22 = bf16[1024,256]{1,0:T(8,128)(2,1)} copy(bf16[1024,256]{1,0:T(8,128)(2,1)} %bitcast.26) | data formatting | bytes 1048576
  113.2 0.0 copy-done.1
  113.2 0.0 copy-start
  113.2 0.8 copy.23
  114.0 0.4 copy-done
  114.4 0.0 copy-start.3
  114.4 0.8 copy.24
  115.2 0.3 copy-done.3
  115.5 0.0 copy-start.2
  115.5 0.7 copy.25
  116.2 0.3 copy-done.2
  116.6 0.7 copy.26
  (3 shorter events, 0.0 us)
Async XLA Ops:
  1.3 0.7 copy-start.4
  1.3 0.7 copy-start.5
  111.3 1.9 %copy-start.1 = (bf16[8,128,256]{2,1,0:T(8,128)(2,1)S(1)}, bf16[8,128,256]{2,1,0:T(8,128)(2,1)}, u32[]{:S(2)}) copy-start(bf16[8,128,256]{2,1,0:T(8,128)(2,1)} %get-tuple-element.13) | copy-start | bytes 1572868
  113.2 1.2 %copy-start = (bf16[8,128,256]{2,1,0:T(8,128)(2,1)S(1)}, bf16[8,128,256]{2,1,0:T(8,128)(2,1)}, u32[]{:S(2)}) copy-start(bf16[8,128,256]{2,1,0:T(8,128)(2,1)} %get-tuple-element.14) | copy-start | bytes 1572868
  114.4 1.1 copy-start.3
  115.5 1.0 copy-start.2
